TPU v7x, 128 devices: a whole 4x4x4 slice. The times are simulated.
128 devices in a mesh: fsdp: 32 (over y, x, core), dp: 4 (over z).
Axes of the slice: x: 4, y: 4, z: 4, core: 2. Of those that a mesh axis runs over, the one named last changes fastest.
Arguments:
- grad_parts: float32 [4, 32, 768, 4096], P('dp', None, None, 'fsdp'), may hold values from -6 to 6
- master: float32 [32, 768, 4096], P(None, 'dp', 'fsdp'), may hold values from -0.21875 to 0.21875
- moment_one: float32 [32, 768, 4096], P(None, 'dp', 'fsdp'), may hold values from -1.2 to 1.2
- moment_two: float32 [32, 768, 4096], P(None, 'dp', 'fsdp'), may hold values from 0.05 to 0.5
- gate_owned: bfloat16 [32, 768, 4096], P('fsdp', 'dp'), may hold values from -0.09375 to 0.09375
- up_owned: bfloat16 [32, 768, 4096], P('fsdp', 'dp'), may hold values from -0.09375 to 0.09375
- tokens: bfloat16 [1024, 4096], P(('fsdp', 'dp')), may hold values from -6 to 6
- expert_ids: int32 [1024, 8], P(('fsdp', 'dp')), may hold values from 0 to 31, all different within a row; in each aligned block of 8 rows (0 to 7, 8 to 15, ...) at most 4 rows name the same one
- gate_values: float32 [1024, 8], P(('fsdp', 'dp')), may hold values from 0.05 to 1
- owner_map: int32 [32], replicated, may hold values from 0 to 31, each once
Outputs:
- owned_down: bfloat16 [32, 768, 4096], P('fsdp', 'dp')
- combined: bfloat16 [1024, 4096], P(('fsdp', 'dp'))
Inputs may be any that keep to these rules, and one draw needn't show every extreme that they name: `expert_ids`: each row names 8 different experts. In each aligned block of 8 rows (the rows of one device) no expert is named by more than 4 rows, a bound that some block reaches. A permutation: expert e is held by index owner_map[e] of fsdp.
All inputs are finite; a program needn't handle non-finite values.
Results may differ from a plain program's by a relative error of at most 0.007.
Values may be sent and summed in bfloat16 or wider, within the bound.
A program may use at most 128 MiB of HBM per device.

v0:
```python
import jax
import jax.numpy as jnp
from jax import lax
from jax.sharding import PartitionSpec as P

beta_one = 0.9
beta_two = 0.95
epsilon = 1e-08
learn_rate = 0.02
decay_rate = 0.1
bias_one = 1.0 - 0.9**10
bias_two = 1.0 - 0.95**10


def expert_part(row_block, gate_mat, up_mat, down_mat):
    width = row_block.shape[-1]
    flat = row_block.reshape(-1, width)
    dims = (((1,), (1,)), ((), ()))
    gate_pre = lax.dot_general(flat, gate_mat, dims, preferred_element_type=jnp.float32)
    up_pre = lax.dot_general(flat, up_mat, dims, preferred_element_type=jnp.float32)
    hidden = (jax.nn.silu(gate_pre) * up_pre).astype(jnp.bfloat16)
    partial_value = jnp.dot(hidden, down_mat, preferred_element_type=jnp.float32)
    return partial_value.reshape(row_block.shape)


def local(
    grad_parts,
    master,
    moment_one,
    moment_two,
    gate_owned,
    up_owned,
    tokens,
    expert_ids,
    gate_values,
    owner_map,
):
    n_fsdp = lax.axis_size("fsdp")
    n_dp = lax.axis_size("dp")
    gradient = lax.psum_scatter(grad_parts, "dp", scatter_dimension=2, tiled=True)[0]
    first_mom = beta_one * moment_one + (1.0 - beta_one) * gradient
    second_mom = beta_two * moment_two + (1.0 - beta_two) * gradient * gradient
    step_dir = first_mom / bias_one / (jnp.sqrt(second_mom / bias_two) + epsilon)
    new_master = master - learn_rate * (step_dir + decay_rate * master)
    new_bf = new_master.astype(jnp.bfloat16)
    experts_n = owner_map.shape[0]
    expert_iota = jnp.arange(experts_n, dtype=jnp.int32)
    holds = owner_map[None, :] == expert_iota[:, None]
    inverse = jnp.sum(jnp.where(holds, expert_iota[None, :], 0), axis=1)
    ordered = jnp.take(new_bf, inverse, axis=0)
    down_mine = lax.all_to_all(ordered, "fsdp", split_axis=0, concat_axis=2, tiled=True)
    tok_dev, picks_row = expert_ids.shape
    width = tokens.shape[1]
    capacity = max(tok_dev // 2, tok_dev * picks_row // experts_n)
    flat_ids = expert_ids.reshape(-1)
    onehot = (flat_ids[:, None] == expert_iota[None, :]).astype(jnp.int32)
    before = jnp.cumsum(onehot, axis=0) - onehot
    slot_rank = jnp.sum(before * onehot, axis=1)
    owner_of = jnp.sum(onehot * owner_map[None, :], axis=1)
    target = owner_of * capacity + slot_rank
    total_rows = n_fsdp * capacity
    matches = (
        target.reshape(tok_dev, picks_row)[None, :, :]
        == jnp.arange(total_rows, dtype=jnp.int32)[:, None, None]
    )
    route_mat = jnp.any(matches, axis=2).astype(jnp.bfloat16)
    outgoing = jnp.dot(route_mat, tokens, preferred_element_type=jnp.float32).astype(jnp.bfloat16)
    outgoing = outgoing.reshape(n_fsdp, capacity, width)
    gate_mat = gate_owned[0]
    up_mat = up_owned[0]
    down_mat = down_mine[0]
    fanned = jnp.broadcast_to(outgoing[:, None], (n_fsdp, n_dp, capacity, width)).reshape(
        n_fsdp * n_dp, capacity, width
    )
    partial_value = expert_part(
        lax.all_to_all(fanned, ("fsdp", "dp"), split_axis=0, concat_axis=0, tiled=True),
        gate_mat,
        up_mat,
        down_mat,
    ).astype(jnp.bfloat16)
    returned = lax.all_to_all(
        partial_value, ("fsdp", "dp"), split_axis=0, concat_axis=0, tiled=True
    )
    returned = returned.reshape(n_fsdp, n_dp, capacity, width).astype(jnp.float32)
    expert_out = jnp.sum(returned, axis=1).astype(jnp.bfloat16)
    flat_out = expert_out.reshape(total_rows, width)
    picked = jnp.take(flat_out, target, axis=0).reshape(tok_dev, picks_row, width)
    combined = jnp.sum(gate_values[:, :, None] * picked.astype(jnp.float32), axis=1).astype(
        jnp.bfloat16
    )
    return (down_mine, combined)


def solution(mesh):
    in_specs = (
        P("dp", None, None, "fsdp"),
        P(None, "dp", "fsdp"),
        P(None, "dp", "fsdp"),
        P(None, "dp", "fsdp"),
        P("fsdp", "dp", None),
        P("fsdp", "dp", None),
        P(("fsdp", "dp"), None),
        P(("fsdp", "dp"), None),
        P(("fsdp", "dp"), None),
        P(),
    )
    out_specs = (P("fsdp", "dp", None), P(("fsdp", "dp"), None))
    return jax.shard_map(local, mesh=mesh, in_specs=in_specs, out_specs=out_specs, check_vma=False)
```

profile of v0, /device:TPU:1, one launch (start us, length us, event | category | flops | bytes accessed | tf_op | source)
XLA Modules:
  0.0 300.5 jit_solution(1461508143781453672)
XLA Ops:
  8.6 1.5 convolution_convert_fusion.1
  10.1 1.5 broadcast_in_dim.51
  11.5 4.1 %broadcast_in_dim.52 = bf16[32,4,4,4096]{3,2,1,0:T(4,128)(2,1)} broadcast(bf16[32,4,4096]{2,1,0:T(4,128)(2,1)S(1)} %broadcast_in_dim.51), dimensions={0,2,3} | broadcast | bytes 5242880 | tf_op jit(solution)/shard_map/broadcast_in_dim | solution.py:72
  15.6 12.0 %all-to-all-start.1 = ((bf16[128,4,4096]{2,1,0:T(4,128)(2,1)}), bf16[128,4,4096]{2,1,0:T(4,128)(2,1)}, u32[]{:S(2)}, u32[]{:S(2)}) async-start(bf16[128,4,4096]{2,1,0:T(4,128)(2,1)} %bitcast.51), calls=%async_computation.2 | async-start | bytes 8388608 | tf_op jit(solution)/shard_map/all_to_all | solution.py:76
  27.7 146.4 %reduce-scatter.2.cloned.1.call-done = f32[1,32,192,128]{3,2,1,0:T(8,128)} async-done(((f32[1,32,768,128]{3,2,1,0:T(8,128)}), f32[1,32,192,128]{3,2,1,0:T(8,128)}) %reduce-scatter.2.cloned.1.call-update) | async-done | bytes 3145744 | tf_op jit(solution)/shard_map/reduce_scatter | solution.py:40
  174.1 5.9 %subtract_convert_fusion = bf16[32,192,128]{2,1,0:T(8,128)(2,1)S(1)} fusion(f32[32,192,128]{2,1,0:T(8,128)} %param.11, f32[1,32,192,128]{3,2,1,0:T(8,128)} %reduce-scatter.2.cloned.1.call-done, f32[32,192,128]{2,1,0:T(8,128)} %param.13, f32[32,192,128]{2,1,0:T(8,128)} %param.12), kind=kLoop, calls=%fused_computation.15 | loop fusion | flops 12582912 | bytes 14155776 | tf_op jit(solution)/shard_map/convert_element_type | solution.py:45
  180.0 1.9 gather_fusion
  181.9 2.8 broadcast_select_fusion
  184.7 6.9 %all-to-all-start = ((bf16[32,192,128]{2,1,0:T(8,128)(2,1)}), bf16[32,192,128]{2,1,0:T(8,128)(2,1)S(1)}, u32[]{:S(2)}, u32[]{:S(2)}) async-start(bf16[32,192,128]{2,1,0:T(8,128)(2,1)} %broadcast_select_fusion), calls=%async_computation.1 | async-start | bytes 3145728 | tf_op jit(solution)/shard_map/all_to_all | solution.py:51
  191.6 6.9 %reshape.95 = bf16[512,4096]{1,0:T(8,128)(2,1)} reshape(bf16[128,4,4096]{2,1,0:T(4,128)(2,1)} %all-to-all-done.1) | data formatting | bytes 8388608 | tf_op jit(solution)/shard_map/reshape | solution.py:17
  198.5 3.9 %fusion.10 = f32[512,192]{0,1:T(8,128)S(1)} fusion(bf16[512,4096]{1,0:T(8,128)(2,1)} %reshape.95, bf16[1,192,4096]{2,1,0:T(8,128)(2,1)S(1)} %copy-done), kind=kOutput, calls=%fused_computation.19 | convolution fusion | flops 805306368 | bytes 6160384 | tf_op jit(solution)/shard_map/dot_general | solution.py:19
  202.4 1.5 fusion.15
  204.2 9.4 %all-to-all-done = bf16[32,192,128]{2,1,0:T(8,128)(2,1)S(1)} async-done(((bf16[32,192,128]{2,1,0:T(8,128)(2,1)}), bf16[32,192,128]{2,1,0:T(8,128)(2,1)S(1)}, u32[]{:S(2)}, u32[]{:S(2)}) %all-to-all-start) | async-done | bytes 1572896 | tf_op jit(solution)/shard_map/all_to_all | solution.py:51
  213.6 1.0 copy.26
  214.7 2.1 reshape.114
  216.7 2.7 convolution_convert_fusion
  219.4 5.2 %copy.30 = bf16[128,4,4096]{2,1,0:T(4,128)(2,1)} copy(bf16[128,4,4096]{2,0,1:T(8,128)(2,1)S(1)} %convolution_convert_fusion) | data formatting | bytes 8388608 | tf_op jit(solution)/shard_map/convert_element_type | solution.py:80
  224.6 6.7 %all-to-all-start.2 = ((bf16[128,4,4096]{2,1,0:T(4,128)(2,1)}), bf16[128,4,4096]{2,1,0:T(4,128)(2,1)}, u32[]{:S(2)}, u32[]{:S(2)}) async-start(bf16[128,4,4096]{2,1,0:T(4,128)(2,1)} %copy.30), calls=%async_computation.3 | async-start | bytes 8388608 | tf_op jit(solution)/shard_map/all_to_all | solution.py:81
  231.3 1.4 copy_bitcast_fusion
  232.7 51.6 %all-to-all-done.2 = bf16[128,4,4096]{2,1,0:T(4,128)(2,1)} async-done(((bf16[128,4,4096]{2,1,0:T(4,128)(2,1)}), bf16[128,4,4096]{2,1,0:T(4,128)(2,1)}, u32[]{:S(2)}, u32[]{:S(2)}) %all-to-all-start.2) | async-done | bytes 4194336 | tf_op jit(solution)/shard_map/all_to_all | solution.py:81
  284.2 6.0 %bitcast_reduce_fusion = bf16[32,4,4096]{2,1,0:T(4,128)(2,1)} fusion(bf16[128,4,4096]{2,1,0:T(4,128)(2,1)} %all-to-all-done.2), kind=kLoop, calls=%fused_computation.5 | loop fusion | flops 1572864 | bytes 5242880 | tf_op jit(solution)/shard_map/reduce_sum | solution.py:85
  290.2 1.5 reshape.97
  291.7 0.9 gather_fusion.1
  292.5 1.1 multiply_reduce_fusion
  (34 shorter events, 1.8 us)
Async XLA Ops:
  7.2 191.3 %copy-start = (bf16[1,192,4096]{2,1,0:T(8,128)(2,1)S(1)}, bf16[1,192,4096]{2,1,0:T(8,128)(2,1)}, u32[]{:S(2)}) copy-start(bf16[1,192,4096]{2,1,0:T(8,128)(2,1)} %param.14) | copy-start | bytes 4718596
  7.2 0.8 copy-start.5
  7.2 1.1 copy-start.6
  7.2 1.4 copy-start.3
  7.2 166.9 %reduce-scatter.2.cloned.1.call-start = ((), (), s32[]{:S(2)}) async-start(), calls=%async_computation.4 | async-start | bytes 15728640 | tf_op jit(solution)/shard_map/reduce_scatter | solution.py:40
  15.6 169.0 %all-to-all-start.1 = ((bf16[128,4,4096]{2,1,0:T(4,128)(2,1)}), bf16[128,4,4096]{2,1,0:T(4,128)(2,1)}, u32[]{:S(2)}, u32[]{:S(2)}) async-start(bf16[128,4,4096]{2,1,0:T(4,128)(2,1)} %bitcast.51), calls=%async_computation.2 | async-start | bytes 8388608 | tf_op jit(solution)/shard_map/all_to_all | solution.py:76
  184.7 29.0 %all-to-all-start = ((bf16[32,192,128]{2,1,0:T(8,128)(2,1)}), bf16[32,192,128]{2,1,0:T(8,128)(2,1)S(1)}, u32[]{:S(2)}, u32[]{:S(2)}) async-start(bf16[32,192,128]{2,1,0:T(8,128)(2,1)} %broadcast_select_fusion), calls=%async_computation.1 | async-start | bytes 3145728 | tf_op jit(solution)/shard_map/all_to_all | solution.py:51
  198.5 3.9 %copy-start.2 = (bf16[512,4096]{1,0:T(8,128)(2,1)S(1)}, bf16[512,4096]{1,0:T(8,128)(2,1)}, u32[]{:S(2)}) copy-start(bf16[512,4096]{1,0:T(8,128)(2,1)} %reshape.95) | copy-start | bytes 12582916
  198.5 3.9 %copy-start.7 = (bf16[1,192,4096]{2,1,0:T(8,128)(2,1)S(1)}, bf16[1,192,4096]{2,1,0:T(8,128)(2,1)}, u32[]{:S(2)}) copy-start(bf16[1,192,4096]{2,1,0:T(8,128)(2,1)} %param.15) | copy-start | bytes 4718596
  224.6 59.6 %all-to-all-start.2 = ((bf16[128,4,4096]{2,1,0:T(4,128)(2,1)}), bf16[128,4,4096]{2,1,0:T(4,128)(2,1)}, u32[]{:S(2)}, u32[]{:S(2)}) async-start(bf16[128,4,4096]{2,1,0:T(4,128)(2,1)} %copy.30), calls=%async_computation.3 | async-start | bytes 8388608 | tf_op jit(solution)/shard_map/all_to_all | solution.py:81
  290.2 2.3 copy-start.4
  290.2 3.4 %copy-start.1 = (bf16[1,192,4096]{2,1,0:T(8,128)(2,1)S(1)}, bf16[1,192,4096]{2,1,0:T(8,128)(2,1)}, u32[]{:S(2)}) copy-start(bf16[1,192,4096]{2,1,0:T(8,128)(2,1)} %param.14) | copy-start | bytes 4718596
Sparse Core Ops, SparseCore 0:
  10.5 163.5 reduce-scatter.1
where the time goes:
time: 301 us; the launch traced here: 300 us
  waiting for transfers between devices  208 us (69%)
  local copies, waits for them, and re-layouts  26.8 us (9%)
  starting transfers between devices  25.6 us (9%)
  other arithmetic  16.3 us (5%)
  between operations  14.2 us (5%)
  matrix products  9.51 us (3%)
    reduce_scatter x1, waiting for transfers between devices, local(): lax.psum_scatter(grad_parts, 'dp', scatter_dimension=2, tiled=True)[0]  146 us
    all_to_all x1, waiting for transfers between devices, local(): lax.all_to_all(partial_value, ('fsdp', 'dp'), split_axis=0, concat_axis=0...  51.6 us
    all_to_all x1, starting transfers between devices, local(): lax.all_to_all(fanned, ('fsdp', 'dp'), split_axis=0, concat_axis=0, tiled...  12 us
    all_to_all x1, waiting for transfers between devices, local(): lax.all_to_all(ordered, 'fsdp', split_axis=0, concat_axis=2, tiled=True)  9.43 us
    all_to_all x1, starting transfers between devices, local(): lax.all_to_all(ordered, 'fsdp', split_axis=0, concat_axis=2, tiled=True)  6.92 us
    reshape x1, local copies, waits for them, and re-layouts, expert_part(): flat = row_block.reshape(-1, width)  6.91 us
    all_to_all x1, starting transfers between devices, local(): lax.all_to_all(partial_value, ('fsdp', 'dp'), split_axis=0, concat_axis=0...  6.66 us
  transfers between devices with their start and end apart: 4, of which 3 were waited for; matrix products, arithmetic and copies ran while one was open for 11% of the time, Pallas kernels for 0%

commit v1 on v0

v1 whole, which is shorter than its diff:
```python
import jax
import jax.numpy as jnp
from jax import lax
from jax.experimental import pallas as pl
from jax.experimental.pallas import tpu as pltpu
from jax.sharding import PartitionSpec as P

MESH = pl.DeviceIdType.MESH

beta_one = 0.9
beta_two = 0.95
epsilon = 1e-08
learn_rate = 0.02
decay_rate = 0.1
bias_one = 1.0 - 0.9**10
bias_two = 1.0 - 0.95**10

NY, NX, NC, NZ = 4, 4, 2, 4
NF = NY * NX * NC
EXPERTS = 32
ROWS = 192
HALF = ROWS // 2
COLS = 128
D = 4096
TOK = 8
CAP = 4
TOKENS = 1024
EXTRA = 128
WIDE = D // 2 + EXTRA
TCOLS = 2 * WIDE
BLK = 256
NBLK = TOKENS // BLK
SLOTS = BLK // TOK * CAP
CHUNKS = 8
PER = EXPERTS // CHUNKS

OFFSETS = (
    ((2, 2), (1, 0)),
    ((2, 1), (1, 2)),
    ((2, 3), (3, 2)),
    ((2, 0), (0, 2)),
    ((1, 1), (3, 3)),
    ((1, 3), (3, 1)),
    ((0, 1), (3, 0)),
    ((0, 3), (0, 0)),
)

BF = jnp.bfloat16
F32 = jnp.float32
NT = (((1,), (1,)), ((), ()))
TN = (((0,), (0,)), ((), ()))
NN = (((1,), (0,)), ((), ()))


def dot(a, b, dims):
    return lax.dot_general(a, b, dims, preferred_element_type=F32)


def adam(g, m, m1, m2):
    first = beta_one * m1 + (1.0 - beta_one) * g
    second = beta_two * m2 + (1.0 - beta_two) * g * g
    step = (first / bias_one) / (jnp.sqrt(second / bias_two) + epsilon)
    return m - learn_rate * (step + decay_rate * m)


def kernel(
    inv, pay, grads, master, mom1, mom2, gate, up,
    owned, combined,
    gb0, gb1, gb2, gb3, st, gu, zb, tok, hb, pos, wrow,
    hs, hr, ds_, dr, fs, fr, wn, acc, zf, zs, zr, zsum, comb,
    lsem, hsem, dsem, fsem, wsem, psem, tsem, asem, zsem, csem,
):
    f = lax.axis_index("fsdp")
    z = lax.axis_index("dp")
    y, x, c = f // 8, lax.rem(f // 2, 4), lax.rem(f, 2)

    def m4(v):
        return lax.rem(v + 4, 4)

    def fid(yy, xx, cc):
        return (yy * 4 + xx) * 2 + cc

    pending = []

    def send(src, dst, sem, i, dev):
        cp = pltpu.make_async_remote_copy(
            src_ref=src, dst_ref=dst, send_sem=sem.at[0, i], recv_sem=sem.at[1, i],
            device_id=dev, device_id_type=MESH,
        )
        cp.start()
        pending.append(cp)

    def arrived(dst, sem, i):
        pltpu.make_async_remote_copy(
            src_ref=dst, dst_ref=dst, send_sem=sem.at[0, i], recv_sem=sem.at[1, i],
            device_id=(f, m4(z + 1)), device_id_type=MESH,
        ).wait_recv()

    gb = (gb0, gb1, gb2, gb3)
    quarter = (m4(z + 2), m4(z + 1), m4(z - 1), z)

    def load_g(k):
        return pltpu.make_async_copy(grads.at[0, :, pl.ds(quarter[k] * ROWS, ROWS), :], gb[k], lsem.at[k])

    loads = [load_g(k) for k in range(4)]
    loads += [pltpu.make_async_copy(r, st.at[k], lsem.at[4 + k]) for k, r in enumerate((master, mom1, mom2))]
    loads += [pltpu.make_async_copy(r.at[0], gu.at[pl.ds(k * ROWS, ROWS)], lsem.at[7 + k]) for k, r in enumerate((gate, up))]
    for cp in loads:
        cp.start()

    barrier = pltpu.get_barrier_semaphore()

    def greet(p, carry):
        pl.semaphore_signal(barrier, inc=1, device_id=(lax.rem(f + p, NF), z), device_id_type=MESH)
        return carry

    lax.fori_loop(1, NF, greet, 0)
    for k in range(1, NZ):
        pl.semaphore_signal(barrier, inc=1, device_id=(f, m4(z + k)), device_id_type=MESH)
    pl.semaphore_wait(barrier, NF - 1 + NZ - 1)

    for k in (2, 1, 3):
        send(pay, zb.at[z], psem, k, (f, m4(z + k)))
    zb[z] = pay[...]

    def owner(j, i):
        dx, dy = OFFSETS[j][i // 2]
        return m4(y + dy), m4(x + dx), lax.rem(c + i % 2, 2)

    def expert(j, i):
        return inv[fid(*owner(j, i))]

    up_z, down_z = (f, m4(z + 1)), (f, m4(z - 1))
    low, high = pl.ds(0, HALF), pl.ds(HALF, HALF)

    def step_h(j):
        for i in range(PER):
            e = expert(j, i)
            hs[0, j, i] = gb[0][e, low, :].astype(BF)
            hs[1, j, i] = gb[0][e, high, :].astype(BF)
        send(hs.at[0, j], hr.at[0, j], hsem, j, up_z)
        send(hs.at[1, j], hr.at[1, j], hsem, CHUNKS + j, down_z)

    def step_d(j):
        for i in range(PER):
            e = expert(j, i)
            ds_[0, j, i] = gb[1][e, high, :].astype(BF)
            ds_[1, j, i] = gb[2][e, low, :].astype(BF)
        send(ds_.at[0, j], dr.at[0, j], dsem, j, up_z)
        send(ds_.at[1, j], dr.at[1, j], dsem, CHUNKS + j, down_z)

    def step_f(j):
        arrived(hr.at[0, j], hsem, j)
        arrived(hr.at[1, j], hsem, CHUNKS + j)
        for i in range(PER):
            e = expert(j, i)
            fs[0, j, i] = (gb[1][e, low, :] + hr[0, j, i].astype(F32)).astype(BF)
            fs[1, j, i] = (gb[2][e, high, :] + hr[1, j, i].astype(F32)).astype(BF)
        send(fs.at[0, j], fr.at[0, j], fsem, j, up_z)
        send(fs.at[1, j], fr.at[1, j], fsem, CHUNKS + j, down_z)

    def step_n(j):
        for k in range(2):
            arrived(fr.at[k, j], fsem, k * CHUNKS + j)
            arrived(dr.at[k, j], dsem, k * CHUNKS + j)
        for i in range(PER):
            e = expert(j, i)
            p = j * PER + i

            def tile(t, carry, e=e, p=p, i=i):
                r = pl.multiple_of(t * 16, 16)
                for k in range(2):
                    rows = pl.ds(k * HALF + r, 16)
                    g = gb[3][e, rows, :] + fr[k, j, i, pl.ds(r, 16), :].astype(F32)
                    g = g + dr[1 - k, j, i, pl.ds(r, 16), :].astype(F32)
                    new = adam(g, st[0, e, rows, :], st[1, e, rows, :], st[2, e, rows, :])
                    wn[p, rows, :] = new.astype(BF)
                return carry

            lax.fori_loop(0, HALF // 16, tile, 0)
            mine = pl.ds(pl.multiple_of(f * COLS, COLS), COLS)
            oy, ox, oc = owner(j, i)
            if OFFSETS[j][i // 2] == (0, 0) and i % 2 == 0:
                cp = pltpu.make_async_copy(wn.at[p], owned.at[0, :, mine], lsem.at[9])
                cp.start()
                own_copy.append(cp)
            else:
                send(wn.at[p], owned.at[0, :, mine], wsem, p, (fid(oy, ox, oc), z))

    own_copy = []

    def gather(buf, sem):
        n_rows, n_cols = buf.shape[-2:]
        halves = (pl.ds(0, n_rows // 2), pl.ds(n_rows // 2, n_rows // 2))
        whole = pl.ds(0, n_cols)
        parts = (pl.ds(0, n_cols // 2), pl.ds(n_cols // 2, n_cols // 2))
        own = ((y, x), (x, y))

        def ref(h, p, s, cols):
            if h == 0:
                return buf.at[p, s, c, halves[0], cols]
            return buf.at[s, p, c, halves[1], cols]

        def dev(h, p, s):
            return (fid(p, s, c), z) if h == 0 else (fid(s, p, c), z)

        def go(h, p, s, cols, i, to):
            r = ref(h, p, s, cols)
            send(r, r, sem, h * 20 + i, dev(h, *to))

        order = (0, -1, 1, 2)

        def secondary(h, k):
            p, s = own[h]
            i = 4 + 4 * order.index(k)
            go(h, m4(p + k), s, whole, i, (p, m4(s + 1)))
            go(h, m4(p + k), s, whole, i + 1, (p, m4(s - 1)))

        def forward(h, k):
            p, s = own[h]
            i = 4 + 4 * order.index(k)
            q = m4(p + k)
            arrived(ref(h, q, m4(s - 1), whole), sem, h * 20 + i)
            go(h, q, m4(s - 1), parts[0], i + 2, (p, m4(s + 1)))
            arrived(ref(h, q, m4(s + 1), whole), sem, h * 20 + i + 1)
            go(h, q, m4(s + 1), parts[1], i + 3, (p, m4(s - 1)))

        for h in (0, 1):
            p, s = own[h]
            go(h, p, s, whole, 0, (m4(p + 1), s))
            go(h, p, s, whole, 1, (m4(p - 1), s))
        for h in (0, 1):
            secondary(h, 0)
        yield
        for h in (0, 1):
            p, s = own[h]
            arrived(ref(h, m4(p - 1), s, whole), sem, h * 20)
            go(h, m4(p - 1), s, parts[0], 2, (m4(p + 1), s))
            secondary(h, -1)
            arrived(ref(h, m4(p + 1), s, whole), sem, h * 20 + 1)
            go(h, m4(p + 1), s, parts[1], 3, (m4(p - 1), s))
            secondary(h, 1)
        yield
        for h in (0, 1):
            forward(h, 0)
        yield
        for h in (0, 1):
            p, s = own[h]
            arrived(ref(h, m4(p + 2), s, parts[0]), sem, h * 20 + 2)
            arrived(ref(h, m4(p + 2), s, parts[1]), sem, h * 20 + 3)
            secondary(h, 2)
        yield
        for h in (0, 1):
            forward(h, -1)
            forward(h, 1)
        yield
        for h in (0, 1):
            forward(h, 2)
        yield
        for h in (0, 1):
            p, s = own[h]
            for k in order:
                i = h * 20 + 4 + 4 * order.index(k)
                arrived(ref(h, m4(p + k), m4(s + 2), parts[0]), sem, i + 2)
                arrived(ref(h, m4(p + k), m4(s + 2), parts[1]), sem, i + 3)
        mine = buf.at[:, :, c]
        send(mine, mine, sem, 40, (fid(y, x, 1 - c), z))
        yield
        arrived(buf.at[:, :, 1 - c], sem, 40)
        yield

    def pack_tokens():
        for k in (1, 3, 2):
            arrived(zb.at[m4(z - k)], psem, k)
        blocks = [zb[k].astype(F32) for k in range(NZ)]
        first = jnp.concatenate([b[0:TOK] for b in blocks], axis=0).astype(BF)
        last = jnp.concatenate([b[TOK : 2 * TOK] for b in blocks], axis=0).astype(BF)
        half = D // 2
        tok[y, x, c, :, 0:half] = first[:, 0:half]
        tok[y, x, c, :, half:D] = last[:, 0:half]
        tok[y, x, c, :, D : D + EXTRA] = first[:, half:WIDE]
        tok[y, x, c, :, D + EXTRA : TCOLS] = last[:, half:WIDE]

    def hidden():
        row = lax.broadcasted_iota(jnp.int32, (EXPERTS, EXTRA), 0)
        lane = lax.broadcasted_iota(jnp.int32, (EXPERTS, EXTRA), 1)
        eye = (row == lane).astype(F32).astype(BF)
        t_row = lax.broadcasted_iota(jnp.int32, (BLK, BLK), 0)
        t_col = lax.broadcasted_iota(jnp.int32, (BLK, BLK), 1)
        before = ((t_row // TOK == t_col // TOK) & (t_row < t_col)).astype(F32).astype(BF)
        base = (lax.broadcasted_iota(jnp.int32, (EXPERTS, BLK), 1) // TOK * CAP).astype(F32)

        def step(b, carry):
            w_hi = dot(eye, tok[b, :, :, :, D : D + EXTRA].reshape(BLK, EXTRA), NT)
            w_lo = dot(eye, tok[b, :, :, :, D + EXTRA : TCOLS].reshape(BLK, EXTRA), NT)
            routed = w_hi > 0.0
            rank = dot(jnp.where(routed, 1.0, 0.0).astype(BF), before, NN)
            pos[b] = jnp.where(routed, rank + base, -1.0)
            wrow[...] = w_hi + w_lo
            pre = dot(gu[...], tok[b, :, :, :, 0:D].reshape(BLK, D), NT)
            g, u = pre[0:ROWS], pre[ROWS : 2 * ROWS]
            h = g / (1.0 + jnp.exp(-g)) * u * wrow[pl.ds(f, 1), :]
            h = dot(h.astype(BF), select(b, f), NT)
            hb[y, x, c, :, pl.ds(pl.multiple_of(b * SLOTS, SLOTS), SLOTS)] = h.astype(BF)
            return carry

        lax.fori_loop(0, NBLK, step, 0)

    def select(b, o):
        slot = lax.broadcasted_iota(jnp.int32, (SLOTS, BLK), 0).astype(F32)
        return jnp.where(slot == pos[b, pl.ds(o, 1), :], 1.0, 0.0).astype(BF)

    def multiply(j, q):
        parts = []
        for i in (2 * q, 2 * q + 1):
            oy, ox, oc = owner(j, i)
            parts.append(dot(wn[j * PER + i], hb[oy, ox, oc], TN).astype(BF))
        for b in range(NBLK):
            cut = slice(b * SLOTS, (b + 1) * SLOTS)
            both = jnp.concatenate([part[:, cut] for part in parts], axis=1)
            sel = jnp.concatenate([select(b, fid(*owner(j, i))) for i in (2 * q, 2 * q + 1)], axis=0)
            acc[:, b * BLK : (b + 1) * BLK] += dot(both, sel, NN)

    loads[0].wait()
    for j in range(CHUNKS):
        step_h(j)
    pack_tokens()
    tokens = gather(tok, tsem)
    next(tokens)
    loads[1].wait()
    loads[2].wait()
    step_d(0)
    step_f(0)
    step_d(1)
    next(tokens)
    step_f(1)
    step_d(2)
    next(tokens)
    step_f(2)
    step_d(3)
    for k in range(3, 9):
        loads[k].wait()
    next(tokens)
    step_n(0)
    step_f(3)
    step_d(4)
    next(tokens)
    step_n(1)
    step_f(4)
    step_d(5)
    next(tokens)
    step_n(2)
    step_f(5)
    step_d(6)
    next(tokens)
    step_f(6)
    step_d(7)
    step_f(7)
    next(tokens)
    hidden()
    hids = gather(hb, asem)
    next(hids)
    step_n(3)
    next(hids)
    step_n(4)
    next(hids)
    step_n(5)
    next(hids)
    step_n(6)
    next(hids)
    step_n(7)
    next(hids)
    next(hids)
    acc[...] = jnp.zeros_like(acc)
    next(hids)
    for j in range(CHUNKS):
        for q in range(2):
            multiply(j, q)

    for b in range(NBLK):
        a = acc[:, b * BLK : (b + 1) * BLK].T.reshape(BLK // (NZ * TOK), NZ, TOK, COLS)
        n = BLK // NZ
        for k in range(NZ):
            part = a[:, k].reshape(n, COLS)
            zf[k, b * n : (b + 1) * n, :] = part
            zs[k, b * n : (b + 1) * n, :] = part.astype(BF)
    for k in (2, 1, 3):
        send(zs.at[m4(z + k)], zr.at[k - 1], zsem, k, (f, m4(z + k)))
    total = zf[z]
    for k in (1, 3, 2):
        arrived(zr.at[k - 1], zsem, k)
        total = total + zr[k - 1].astype(F32)
    zsum[...] = total

    def out_copy(p, to):
        return pltpu.make_async_remote_copy(
            src_ref=zsum.at[pl.ds(pl.multiple_of(to * TOK, TOK), TOK)], dst_ref=comb.at[f],
            send_sem=csem.at[0, p], recv_sem=csem.at[1, p], device_id=(to, z), device_id_type=MESH,
        )

    def out_send(p, carry):
        out_copy(p, lax.rem(f + p, NF)).start()
        return carry

    lax.fori_loop(1, NF, out_send, 0)
    comb[f] = zsum[pl.ds(pl.multiple_of(f * TOK, TOK), TOK), :]

    def out_wait(p, carry):
        src = lax.rem(f - p + NF, NF)
        pltpu.make_async_remote_copy(
            src_ref=comb.at[src], dst_ref=comb.at[src], send_sem=csem.at[0, p], recv_sem=csem.at[1, p],
            device_id=(lax.rem(f + p, NF), z), device_id_type=MESH,
        ).wait_recv()
        out_copy(p, lax.rem(f + p, NF)).wait_send()
        return carry

    lax.fori_loop(1, NF, out_wait, 0)
    for k in range(NF):
        combined[:, k * COLS : (k + 1) * COLS] = comb[k].astype(BF)

    for j in range(CHUNKS):
        for i in range(PER):
            dx, dy = OFFSETS[j][i // 2]
            if (dx, dy) == (0, 0) and i % 2 == 0:
                continue
            src = fid(m4(y - dy), m4(x - dx), lax.rem(c + i % 2, 2))
            arrived(owned.at[0, :, pl.ds(pl.multiple_of(src * COLS, COLS), COLS)], wsem, j * PER + i)
    for cp in own_copy:
        cp.wait()
    for cp in pending:
        cp.wait_send()


def local(grad_parts, master, moment_one, moment_two, gate_owned, up_owned, tokens, expert_ids, gate_values, owner_map):
    index = jnp.arange(EXPERTS, dtype=jnp.int32)
    inverse = jnp.sum(jnp.where(owner_map[None, :] == index[:, None], index[None, :], 0), axis=1)
    weight = jnp.sum(
        jnp.where(expert_ids[:, :, None] == inverse[None, None, :], gate_values[:, :, None], 0.0), axis=1
    )
    w_hi = lax.reduce_precision(weight, 8, 7)
    w_lo = lax.reduce_precision(weight - w_hi, 8, 7)
    extra = jnp.concatenate([w_hi, w_lo], axis=0).astype(BF)
    extra = jnp.pad(extra, ((0, 0), (0, EXTRA - EXPERTS)))
    half = D // 2
    pay = jnp.concatenate([jnp.concatenate([tokens[:, :half], tokens[:, half:]], axis=0), extra], axis=1)
    vmem = pl.BlockSpec(memory_space=pltpu.VMEM)
    hbm = pl.BlockSpec(memory_space=pl.ANY)
    dma = pltpu.SemaphoreType.DMA
    ring = (2, CHUNKS, PER, HALF, COLS)
    return pl.pallas_call(
        kernel,
        out_shape=(
            jax.ShapeDtypeStruct((1, ROWS, D), BF),
            jax.ShapeDtypeStruct((TOK, D), BF),
        ),
        in_specs=[pl.BlockSpec(memory_space=pltpu.SMEM), vmem] + [hbm] * 6,
        out_specs=(hbm, vmem),
        scratch_shapes=[
            pltpu.VMEM((EXPERTS, ROWS, COLS), F32),
            pltpu.VMEM((EXPERTS, ROWS, COLS), F32),
            pltpu.VMEM((EXPERTS, ROWS, COLS), F32),
            pltpu.VMEM((EXPERTS, ROWS, COLS), F32),
            pltpu.VMEM((3, EXPERTS, ROWS, COLS), F32),
            pltpu.VMEM((2 * ROWS, D), BF),
            pltpu.VMEM((NZ, 2 * TOK, WIDE), BF),
            pltpu.VMEM((NY, NX, NC, NZ * TOK, TCOLS), BF),
            pltpu.VMEM((NY, NX, NC, ROWS, NBLK * SLOTS), BF),
            pltpu.VMEM((NBLK, EXPERTS, BLK), F32),
            pltpu.VMEM((EXPERTS, BLK), F32),
            pltpu.VMEM(ring, BF),
            pltpu.VMEM(ring, BF),
            pltpu.VMEM(ring, BF),
            pltpu.VMEM(ring, BF),
            pltpu.VMEM(ring, BF),
            pltpu.VMEM(ring, BF),
            pltpu.VMEM((EXPERTS, ROWS, COLS), BF),
            pltpu.VMEM((COLS, TOKENS), F32),
            pltpu.VMEM((NZ, TOKENS // NZ, COLS), F32),
            pltpu.VMEM((NZ, TOKENS // NZ, COLS), BF),
            pltpu.VMEM((NZ - 1, TOKENS // NZ, COLS), BF),
            pltpu.VMEM((TOKENS // NZ, COLS), F32),
            pltpu.VMEM((NF, TOK, COLS), F32),
            dma((10,)),
            dma((2, 2 * CHUNKS)),
            dma((2, 2 * CHUNKS)),
            dma((2, 2 * CHUNKS)),
            dma((2, EXPERTS)),
            dma((2, NZ)),
            dma((2, 41)),
            dma((2, 41)),
            dma((2, NZ)),
            dma((2, NF)),
        ],
        compiler_params=pltpu.CompilerParams(
            collective_id=0, has_side_effects=True, vmem_limit_bytes=60 * 2**20
        ),
    )(inverse, pay, grad_parts, master, moment_one, moment_two, gate_owned, up_owned)


def solution(mesh):
    in_specs = (
        P("dp", None, None, "fsdp"),
        P(None, "dp", "fsdp"),
        P(None, "dp", "fsdp"),
        P(None, "dp", "fsdp"),
        P("fsdp", "dp", None),
        P("fsdp", "dp", None),
        P(("fsdp", "dp"), None),
        P(("fsdp", "dp"), None),
        P(("fsdp", "dp"), None),
        P(),
    )
    out_specs = (P("fsdp", "dp", None), P(("fsdp", "dp"), None))
    return jax.shard_map(local, mesh=mesh, in_specs=in_specs, out_specs=out_specs, check_vma=False)
```

time: 301 us -> 122 us (0.41)
  waiting for transfers between devices: 208 us -> 0 us
  Pallas kernels: 0 us -> 115 us
  starting transfers between devices: 25.6 us -> 0 us
  local copies, waits for them, and re-layouts: 26.8 us -> 4.15 us
  other arithmetic: 16.3 us -> 2.21 us
  between operations: 14.2 us -> 0.68 us
  matrix products: 9.51 us -> 0 us
    reduce_scatter x1 -> x0, waiting for transfers between devices: 146 us -> none  [local(): lax.psum_scatter(grad_parts, 'dp', scatter_dimension=2, tiled=True)[0]]
    pallas_call x0 -> x1, Pallas kernels: none -> 115 us  [local(): pl.pallas_call(kernel, out_shape=(jax.ShapeDtypeStruct((1, ROWS, D), BF),...]
    all_to_all x3 -> x0, waiting for transfers between devices: 61 us -> none  [the longest x1 51.6 us: local(): lax.all_to_all(partial_value, ('fsdp', 'dp'), split_axis=0, concat_axis=0...]
    all_to_all x3 -> x0, starting transfers between devices: 25.5 us -> none  [the longest x1 12 us: local(): lax.all_to_all(fanned, ('fsdp', 'dp'), split_axis=0, concat_axis=0, tiled...]
    dot_general x4 -> x0, matrix products: 9.51 us -> none  [the longest x1 3.87 us: expert_part(): lax.dot_general(flat, gate_mat, dims, preferred_element_type=jnp.float32)]
    reshape x2 -> x0, local copies, waits for them, and re-layouts: 8.37 us -> none  [the longest x1 6.91 us: expert_part(): flat = row_block.reshape(-1, width)]
    convert_element_type x2 -> x0, other arithmetic: 5.95 us -> none  [the longest x1 5.88 us: local(): new_bf = new_master.astype(jnp.bfloat16)]
    reduce_sum x4 -> x2, other arithmetic: 7.31 us -> 1.56 us  [the longest x1 0.79 us: local(): jnp.sum(jnp.where(expert_ids[:, :, None] == inverse[None, None, :], gate_...]
  transfers between devices with their start and end apart: 4 -> 0, of which waited for: 3 -> 0; matrix products, arithmetic and copies ran while one was open for 11% -> 0% of each run, Pallas kernels for 0% -> 0%
where the time goes in v1:
time: 122 us
  Pallas kernels  115 us (94%)
  local copies, waits for them, and re-layouts  4.15 us (3%)
  other arithmetic  2.21 us (2%)
    pallas_call x1, Pallas kernels, local(): pl.pallas_call(kernel, out_shape=(jax.ShapeDtypeStruct((1, ROWS, D), BF),...  115 us
    unnamed x6, local copies, waits for them, and re-layouts  3.37 us

profile of v1, /device:TPU:1, one launch (start us, length us, event | category | flops | bytes accessed | tf_op | source)
XLA Modules:
  0.0 122.2 jit_solution(7210982645135243317)
XLA Ops:
  0.6 0.8 select_reduce_fusion.1.inv
  1.4 0.0 copy-start.1
  1.4 0.8 select_reduce_fusion
  2.2 0.8 fusion.5
  3.0 0.6 pad_maximum_fusion.pay
  3.7 0.0 copy-done.1
  3.7 115.1 %shard_map.113 = (bf16[1,192,4096]{2,1,0:T(8,128)(2,1)}, bf16[8,4096]{1,0:T(8,128)(2,1)}) custom-call(s32[32]{0:T(128)} %copy-done.1, bf16[16,2176]{1,0:T(8,128)(2,1)} %pad_maximum_fusion.pay, f32[1,32,768,128]{3,2,1,0:T(8,128)} %grads.1, f32[32,192,128]{2,1,0:T(8,128)} %master.1, f32[32,192,128]{2,1,0:T(8,128)} %mom1.1, f32[32,192,128]{2,1,0:T(8,128)} %mom2.1, ...), custom_call_target="tpu_custom_call" | custom-call | tf_op jit(solution)/shard_map/pallas_call | solution.py:450
  118.8 0.0 copy-start
  118.8 2.7 %copy.14 = bf16[1,192,4096]{2,1,0:T(8,128)(2,1)} copy(bf16[1,192,4096]{2,1,0:T(8,128)(2,1)} %get-tuple-element.8) | data formatting | bytes 3145728
  121.6 0.0 copy-done
  121.6 0.6 copy.15
  (2 shorter events, 0.0 us)
Async XLA Ops:
  1.4 2.3 %copy-start.1 = (s32[32]{0:T(128)}, s32[32]{0:T(128)S(1)}, u32[]{:S(2)}) copy-start(s32[32]{0:T(128)S(1)} %select_reduce_fusion.1.inv) | copy-start | bytes 388
  118.8 2.7 %copy-start = (bf16[8,4096]{1,0:T(8,128)(2,1)S(1)}, bf16[8,4096]{1,0:T(8,128)(2,1)}, u32[]{:S(2)}) copy-start(bf16[8,4096]{1,0:T(8,128)(2,1)} %get-tuple-element.9) | copy-start | bytes 196612

commit v2 on v1

--- a/solution.py
+++ b/solution.py
@@ -64,9 +64,9 @@
 
 
 def kernel(
-    inv, pay, grads, master, mom1, mom2, gate, up,
+    omap, tokens, ids, gates, grads, master, mom1, mom2, gate, up,
     owned, combined,
-    gb0, gb1, gb2, gb3, st, gu, zb, tok, hb, pos, wrow,
+    inv, gb0, gb1, gb2, gb3, st, gu, pay, zb, tok, hb, pos, wrow,
     hs, hr, ds_, dr, fs, fr, wn, acc, zf, zs, zr, zsum, comb,
     lsem, hsem, dsem, fsem, wsem, psem, tsem, asem, zsem, csem,
 ):
@@ -105,19 +105,38 @@
     loads = [load_g(k) for k in range(4)]
     loads += [pltpu.make_async_copy(r, st.at[k], lsem.at[4 + k]) for k, r in enumerate((master, mom1, mom2))]
     loads += [pltpu.make_async_copy(r.at[0], gu.at[pl.ds(k * ROWS, ROWS)], lsem.at[7 + k]) for k, r in enumerate((gate, up))]
-    for cp in loads:
+    for cp in loads[0:3]:
         cp.start()
 
     barrier = pltpu.get_barrier_semaphore()
 
-    def greet(p, carry):
-        pl.semaphore_signal(barrier, inc=1, device_id=(lax.rem(f + p, NF), z), device_id_type=MESH)
-        return carry
-
-    lax.fori_loop(1, NF, greet, 0)
+    for near in (fid(y, x, 1 - c), fid(y, m4(x + 1), c), fid(y, m4(x - 1), c), fid(m4(y + 1), x, c), fid(m4(y - 1), x, c)):
+        pl.semaphore_signal(barrier, inc=1, device_id=(near, z), device_id_type=MESH)
     for k in range(1, NZ):
         pl.semaphore_signal(barrier, inc=1, device_id=(f, m4(z + k)), device_id_type=MESH)
-    pl.semaphore_wait(barrier, NF - 1 + NZ - 1)
+
+    lane = lax.broadcasted_iota(jnp.int32, (TOK, EXTRA), 1)
+    invrow = jnp.full((TOK, EXTRA), -1, jnp.int32)
+    for e in range(EXPERTS):
+        invrow = jnp.where(lane == omap[e], e, invrow)
+    weight = jnp.zeros((TOK, EXTRA), F32)
+    for k in range(TOK):
+        weight += jnp.where(ids[:, k : k + 1] == invrow, gates[:, k : k + 1], 0.0)
+    w_hi = weight.astype(BF).astype(F32)
+    half_d = D // 2
+    rows = tokens[...].astype(F32)
+    pay[:, 0:half_d] = jnp.concatenate([rows[:, 0:half_d], rows[:, half_d:D]], axis=0).astype(BF)
+    pay[:, half_d:WIDE] = jnp.concatenate([w_hi, weight - w_hi], axis=0).astype(BF)
+
+    def invert(o, carry):
+        found = 0
+        for e in range(EXPERTS):
+            found = jnp.where(omap[e] == o, e, found)
+        inv[o] = found
+        return carry
+
+    lax.fori_loop(0, EXPERTS, invert, 0)
+    pl.semaphore_wait(barrier, NZ - 1 + 5)
 
     for k in (2, 1, 3):
         send(pay, zb.at[z], psem, k, (f, m4(z + k)))
@@ -129,6 +148,10 @@
 
     def expert(j, i):
         return inv[fid(*owner(j, i))]
+
+    def place(j, i):
+        dx, dy = OFFSETS[j][i // 2]
+        return (dy * 4 + dx) * 2 + i % 2
 
     up_z, down_z = (f, m4(z + 1)), (f, m4(z - 1))
     low, high = pl.ds(0, HALF), pl.ds(HALF, HALF)
@@ -165,7 +188,7 @@
             arrived(dr.at[k, j], dsem, k * CHUNKS + j)
         for i in range(PER):
             e = expert(j, i)
-            p = j * PER + i
+            p = place(j, i)
 
             def tile(t, carry, e=e, p=p, i=i):
                 r = pl.multiple_of(t * 16, 16)
@@ -178,14 +201,17 @@
                 return carry
 
             lax.fori_loop(0, HALF // 16, tile, 0)
-            mine = pl.ds(pl.multiple_of(f * COLS, COLS), COLS)
-            oy, ox, oc = owner(j, i)
-            if OFFSETS[j][i // 2] == (0, 0) and i % 2 == 0:
+
+    def step_w(j):
+        mine = pl.ds(pl.multiple_of(f * COLS, COLS), COLS)
+        for i in range(PER):
+            p = place(j, i)
+            if p == 0:
                 cp = pltpu.make_async_copy(wn.at[p], owned.at[0, :, mine], lsem.at[9])
                 cp.start()
                 own_copy.append(cp)
             else:
-                send(wn.at[p], owned.at[0, :, mine], wsem, p, (fid(oy, ox, oc), z))
+                send(wn.at[p], owned.at[0, :, mine], wsem, p, (fid(*owner(j, i)), z))
 
     own_copy = []
 
@@ -225,12 +251,26 @@
             arrived(ref(h, q, m4(s + 1), whole), sem, h * 20 + i + 1)
             go(h, q, m4(s + 1), parts[1], i + 3, (p, m4(s - 1)))
 
+        sent = []
+
+        def share(h, p, s):
+            i = 40 + len(sent)
+            r = ref(h, p, s, whole)
+            send(r, r, sem, i, (fid(y, x, 1 - c), z))
+            other = buf.at[p, s, 1 - c, halves[0]] if h == 0 else buf.at[s, p, 1 - c, halves[1]]
+            sent.append((other, i))
+
+        def shared(first, last):
+            for other, i in sent[first:last]:
+                arrived(other, sem, i)
+
         for h in (0, 1):
             p, s = own[h]
             go(h, p, s, whole, 0, (m4(p + 1), s))
             go(h, p, s, whole, 1, (m4(p - 1), s))
         for h in (0, 1):
             secondary(h, 0)
+            share(h, *own[h])
         yield
         for h in (0, 1):
             p, s = own[h]
@@ -242,7 +282,11 @@
             secondary(h, 1)
         yield
         for h in (0, 1):
+            p, s = own[h]
             forward(h, 0)
+            for k in (-1, 1):
+                share(h, m4(p + k), s)
+                share(h, p, m4(s + k))
         yield
         for h in (0, 1):
             p, s = own[h]
@@ -251,22 +295,31 @@
             secondary(h, 2)
         yield
         for h in (0, 1):
-            forward(h, -1)
-            forward(h, 1)
-        yield
-        for h in (0, 1):
+            p, s = own[h]
+            for k in (-1, 1):
+                forward(h, k)
+                share(h, m4(p + k), m4(s - 1))
+                share(h, m4(p + k), m4(s + 1))
+        near = len(sent)
+        yield
+        for h in (0, 1):
+            p, s = own[h]
+            share(h, m4(p + 2), s)
             forward(h, 2)
-        yield
+            share(h, m4(p + 2), m4(s - 1))
+            share(h, m4(p + 2), m4(s + 1))
+        shared(0, near)
+        yield
+        far = len(sent)
         for h in (0, 1):
             p, s = own[h]
             for k in order:
                 i = h * 20 + 4 + 4 * order.index(k)
                 arrived(ref(h, m4(p + k), m4(s + 2), parts[0]), sem, i + 2)
                 arrived(ref(h, m4(p + k), m4(s + 2), parts[1]), sem, i + 3)
-        mine = buf.at[:, :, c]
-        send(mine, mine, sem, 40, (fid(y, x, 1 - c), z))
-        yield
-        arrived(buf.at[:, :, 1 - c], sem, 40)
+                share(h, m4(p + k), m4(s + 2))
+        shared(near, far)
+        shared(far, len(sent))
         yield
 
     def pack_tokens():
@@ -310,72 +363,97 @@
         slot = lax.broadcasted_iota(jnp.int32, (SLOTS, BLK), 0).astype(F32)
         return jnp.where(slot == pos[b, pl.ds(o, 1), :], 1.0, 0.0).astype(BF)
 
-    def multiply(j, q):
-        parts = []
-        for i in (2 * q, 2 * q + 1):
-            oy, ox, oc = owner(j, i)
-            parts.append(dot(wn[j * PER + i], hb[oy, ox, oc], TN).astype(BF))
+    def multiply(dx, dy):
+        oy, ox = m4(y + dy), m4(x + dx)
+        parts, owners = [], []
+        for dc in range(NC):
+            oc = lax.rem(c + dc, 2)
+            owners.append(fid(oy, ox, oc))
+            parts.append(dot(wn[(dy * 4 + dx) * 2 + dc], hb[oy, ox, oc], TN).astype(BF))
         for b in range(NBLK):
             cut = slice(b * SLOTS, (b + 1) * SLOTS)
             both = jnp.concatenate([part[:, cut] for part in parts], axis=1)
-            sel = jnp.concatenate([select(b, fid(*owner(j, i))) for i in (2 * q, 2 * q + 1)], axis=0)
+            sel = jnp.concatenate([select(b, o) for o in owners], axis=0)
             acc[:, b * BLK : (b + 1) * BLK] += dot(both, sel, NN)
+
+    def skip(d):
+        return d + d // 2
+
+    def multiply_near(n, carry):
+        multiply(skip(n % 3), skip(n // 3))
+        return carry
+
+    def multiply_row(n, carry):
+        multiply(n, 2)
+        return carry
+
+    def multiply_column(n, carry):
+        multiply(2, skip(n))
+        return carry
 
     loads[0].wait()
     for j in range(CHUNKS):
         step_h(j)
     pack_tokens()
-    tokens = gather(tok, tsem)
-    next(tokens)
+    tokens_all = gather(tok, tsem)
+    next(tokens_all)
+    for k in range(3, 9):
+        loads[k].start()
     loads[1].wait()
     loads[2].wait()
     step_d(0)
+    step_d(1)
     step_f(0)
-    step_d(1)
-    next(tokens)
+    next(tokens_all)
     step_f(1)
     step_d(2)
-    next(tokens)
+    next(tokens_all)
     step_f(2)
     step_d(3)
+    next(tokens_all)
     for k in range(3, 9):
         loads[k].wait()
-    next(tokens)
-    step_n(0)
     step_f(3)
     step_d(4)
-    next(tokens)
-    step_n(1)
     step_f(4)
     step_d(5)
-    next(tokens)
-    step_n(2)
+    next(tokens_all)
     step_f(5)
     step_d(6)
-    next(tokens)
+    step_n(0)
+    next(tokens_all)
     step_f(6)
     step_d(7)
     step_f(7)
-    next(tokens)
+    next(tokens_all)
+    step_w(0)
     hidden()
     hids = gather(hb, asem)
     next(hids)
+    step_n(1)
+    next(hids)
+    step_n(2)
+    next(hids)
     step_n(3)
     next(hids)
     step_n(4)
     next(hids)
+    step_w(1)
+    step_w(2)
     step_n(5)
     next(hids)
+    step_w(3)
+    step_w(4)
+    step_w(5)
     step_n(6)
-    next(hids)
+    step_w(6)
     step_n(7)
-    next(hids)
-    next(hids)
+    step_w(7)
     acc[...] = jnp.zeros_like(acc)
-    next(hids)
-    for j in range(CHUNKS):
-        for q in range(2):
-            multiply(j, q)
+    lax.fori_loop(0, 9, multiply_near, 0)
+    next(hids)
+    lax.fori_loop(0, 4, multiply_row, 0)
+    lax.fori_loop(0, 3, multiply_column, 0)
 
     for b in range(NBLK):
         a = acc[:, b * BLK : (b + 1) * BLK].T.reshape(BLK // (NZ * TOK), NZ, TOK, COLS)
@@ -424,7 +502,7 @@
             if (dx, dy) == (0, 0) and i % 2 == 0:
                 continue
             src = fid(m4(y - dy), m4(x - dx), lax.rem(c + i % 2, 2))
-            arrived(owned.at[0, :, pl.ds(pl.multiple_of(src * COLS, COLS), COLS)], wsem, j * PER + i)
+            arrived(owned.at[0, :, pl.ds(pl.multiple_of(src * COLS, COLS), COLS)], wsem, place(j, i))
     for cp in own_copy:
         cp.wait()
     for cp in pending:
@@ -432,17 +510,6 @@
 
 
 def local(grad_parts, master, moment_one, moment_two, gate_owned, up_owned, tokens, expert_ids, gate_values, owner_map):
-    index = jnp.arange(EXPERTS, dtype=jnp.int32)
-    inverse = jnp.sum(jnp.where(owner_map[None, :] == index[:, None], index[None, :], 0), axis=1)
-    weight = jnp.sum(
-        jnp.where(expert_ids[:, :, None] == inverse[None, None, :], gate_values[:, :, None], 0.0), axis=1
-    )
-    w_hi = lax.reduce_precision(weight, 8, 7)
-    w_lo = lax.reduce_precision(weight - w_hi, 8, 7)
-    extra = jnp.concatenate([w_hi, w_lo], axis=0).astype(BF)
-    extra = jnp.pad(extra, ((0, 0), (0, EXTRA - EXPERTS)))
-    half = D // 2
-    pay = jnp.concatenate([jnp.concatenate([tokens[:, :half], tokens[:, half:]], axis=0), extra], axis=1)
     vmem = pl.BlockSpec(memory_space=pltpu.VMEM)
     hbm = pl.BlockSpec(memory_space=pl.ANY)
     dma = pltpu.SemaphoreType.DMA
@@ -453,15 +520,17 @@
             jax.ShapeDtypeStruct((1, ROWS, D), BF),
             jax.ShapeDtypeStruct((TOK, D), BF),
         ),
-        in_specs=[pl.BlockSpec(memory_space=pltpu.SMEM), vmem] + [hbm] * 6,
+        in_specs=[pl.BlockSpec(memory_space=pltpu.SMEM)] + [vmem] * 3 + [hbm] * 6,
         out_specs=(hbm, vmem),
         scratch_shapes=[
+            pltpu.SMEM((EXPERTS,), jnp.int32),
             pltpu.VMEM((EXPERTS, ROWS, COLS), F32),
             pltpu.VMEM((EXPERTS, ROWS, COLS), F32),
             pltpu.VMEM((EXPERTS, ROWS, COLS), F32),
             pltpu.VMEM((EXPERTS, ROWS, COLS), F32),
             pltpu.VMEM((3, EXPERTS, ROWS, COLS), F32),
             pltpu.VMEM((2 * ROWS, D), BF),
+            pltpu.VMEM((2 * TOK, WIDE), BF),
             pltpu.VMEM((NZ, 2 * TOK, WIDE), BF),
             pltpu.VMEM((NY, NX, NC, NZ * TOK, TCOLS), BF),
             pltpu.VMEM((NY, NX, NC, ROWS, NBLK * SLOTS), BF),
@@ -486,15 +555,15 @@
             dma((2, 2 * CHUNKS)),
             dma((2, EXPERTS)),
             dma((2, NZ)),
-            dma((2, 41)),
-            dma((2, 41)),
+            dma((2, 72)),
+            dma((2, 72)),
             dma((2, NZ)),
             dma((2, NF)),
         ],
         compiler_params=pltpu.CompilerParams(
             collective_id=0, has_side_effects=True, vmem_limit_bytes=60 * 2**20
         ),
-    )(inverse, pay, grad_parts, master, moment_one, moment_two, gate_owned, up_owned)
+    )(owner_map, tokens, expert_ids, gate_values, grad_parts, master, moment_one, moment_two, gate_owned, up_owned)
 
 
 def solution(mesh):

time: 122 us -> 103 us (0.84)
  Pallas kernels: 115 us -> 99.1 us
  other arithmetic: 2.21 us -> 0 us
    pallas_call x1, Pallas kernels: 115 us -> 99.1 us  [local(): pl.pallas_call(kernel, out_shape=(jax.ShapeDtypeStruct((1, ROWS, D), BF),...]
    reduce_sum x2 -> x0, other arithmetic: 1.56 us -> none  [the longest x1 0.79 us: local(): jnp.sum(jnp.where(expert_ids[:, :, None] == inverse[None, None, :], gate_...]
    unnamed x6 -> x4, local copies, waits for them, and re-layouts: 3.37 us -> 3.37 us
where the time goes in v2:
time: 103 us
  Pallas kernels  99.1 us (96%)
  local copies, waits for them, and re-layouts  3.37 us (3%)
    pallas_call x1, Pallas kernels, local(): pl.pallas_call(kernel, out_shape=(jax.ShapeDtypeStruct((1, ROWS, D), BF),...  99.1 us
    unnamed x4, local copies, waits for them, and re-layouts  3.37 us

profile of v2, /device:TPU:1, one launch (start us, length us, event | category | flops | bytes accessed | tf_op | source)
XLA Modules:
  0.0 103.1 jit_solution(11618936332871820826)
XLA Ops:
  0.6 99.1 %shard_map.113 = (bf16[1,192,4096]{2,1,0:T(8,128)(2,1)}, bf16[8,4096]{1,0:T(8,128)(2,1)}) custom-call(s32[32]{0:T(128)} %omap.1, bf16[8,4096]{1,0:T(8,128)(2,1)} %tokens.1, s32[8,8]{1,0:T(8,128)} %ids.1, f32[8,8]{1,0:T(8,128)} %gates.1, f32[1,32,768,128]{3,2,1,0:T(8,128)} %grads.1, f32[32,192,128]{2,1,0:T(8,128)} %master.1, f32[32,192,128]{2,1,0:T(8,128)} %mom1.1, ...), custom_call_target="tpu_custom_call" | custom-call | tf_op jit(solution)/shard_map/pallas_call | solution.py:517
  99.7 0.0 copy-start
  99.7 2.7 %copy.14 = bf16[1,192,4096]{2,1,0:T(8,128)(2,1)} copy(bf16[1,192,4096]{2,1,0:T(8,128)(2,1)} %get-tuple-element.4) | data formatting | bytes 3145728
  102.5 0.0 copy-done
  102.5 0.6 copy.15
Async XLA Ops:
  99.7 2.7 %copy-start = (bf16[8,4096]{1,0:T(8,128)(2,1)S(1)}, bf16[8,4096]{1,0:T(8,128)(2,1)}, u32[]{:S(2)}) copy-start(bf16[8,4096]{1,0:T(8,128)(2,1)} %get-tuple-element.5) | copy-start | bytes 196612

commit v3 on v2

--- a/solution.py
+++ b/solution.py
@@ -391,14 +391,14 @@
         multiply(2, skip(n))
         return carry
 
+    for k in range(3, 9):
+        loads[k].start()
     loads[0].wait()
     for j in range(CHUNKS):
         step_h(j)
     pack_tokens()
     tokens_all = gather(tok, tsem)
     next(tokens_all)
-    for k in range(3, 9):
-        loads[k].start()
     loads[1].wait()
     loads[2].wait()
     step_d(0)
@@ -411,8 +411,6 @@
     step_f(2)
     step_d(3)
     next(tokens_all)
-    for k in range(3, 9):
-        loads[k].wait()
     step_f(3)
     step_d(4)
     step_f(4)
@@ -420,13 +418,14 @@
     next(tokens_all)
     step_f(5)
     step_d(6)
+    for k in range(3, 9):
+        loads[k].wait()
     step_n(0)
     next(tokens_all)
     step_f(6)
     step_d(7)
     step_f(7)
     next(tokens_all)
-    step_w(0)
     hidden()
     hids = gather(hb, asem)
     next(hids)
@@ -438,22 +437,23 @@
     next(hids)
     step_n(4)
     next(hids)
+    step_n(5)
+    next(hids)
+    step_w(0)
     step_w(1)
+    step_n(6)
+    step_n(7)
+    acc[...] = jnp.zeros_like(acc)
+    lax.fori_loop(0, 9, multiply_near, 0, unroll=3)
     step_w(2)
-    step_n(5)
-    next(hids)
     step_w(3)
     step_w(4)
     step_w(5)
-    step_n(6)
+    next(hids)
     step_w(6)
-    step_n(7)
     step_w(7)
-    acc[...] = jnp.zeros_like(acc)
-    lax.fori_loop(0, 9, multiply_near, 0)
-    next(hids)
-    lax.fori_loop(0, 4, multiply_row, 0)
-    lax.fori_loop(0, 3, multiply_column, 0)
+    lax.fori_loop(0, 4, multiply_row, 0, unroll=2)
+    lax.fori_loop(0, 3, multiply_column, 0, unroll=3)
 
     for b in range(NBLK):
         a = acc[:, b * BLK : (b + 1) * BLK].T.reshape(BLK // (NZ * TOK), NZ, TOK, COLS)

time: 103 us -> 97.8 us (0.950)
  Pallas kernels: 99.1 us -> 93.6 us
    pallas_call x1, Pallas kernels: 99.1 us -> 93.6 us  [local(): pl.pallas_call(kernel, out_shape=(jax.ShapeDtypeStruct((1, ROWS, D), BF),...]
where the time goes in v3:
time: 97.8 us; the launch traced here: 97.6 us
  Pallas kernels  93.6 us (96%)
  local copies, waits for them, and re-layouts  3.37 us (3%)
    pallas_call x1, Pallas kernels, local(): pl.pallas_call(kernel, out_shape=(jax.ShapeDtypeStruct((1, ROWS, D), BF),...  93.6 us
    unnamed x4, local copies, waits for them, and re-layouts  3.37 us

profile of v3, /device:TPU:1, one launch (start us, length us, event | category | flops | bytes accessed | tf_op | source)
XLA Modules:
  0.0 97.6 jit_solution(10193840044732337528)
XLA Ops:
  0.6 93.6 %shard_map.113 = (bf16[1,192,4096]{2,1,0:T(8,128)(2,1)}, bf16[8,4096]{1,0:T(8,128)(2,1)}) custom-call(s32[32]{0:T(128)} %omap.1, bf16[8,4096]{1,0:T(8,128)(2,1)} %tokens.1, s32[8,8]{1,0:T(8,128)} %ids.1, f32[8,8]{1,0:T(8,128)} %gates.1, f32[1,32,768,128]{3,2,1,0:T(8,128)} %grads.1, f32[32,192,128]{2,1,0:T(8,128)} %master.1, f32[32,192,128]{2,1,0:T(8,128)} %mom1.1, ...), custom_call_target="tpu_custom_call" | custom-call | tf_op jit(solution)/shard_map/pallas_call | solution.py:517
  94.3 0.0 copy-start
  94.3 2.7 %copy.14 = bf16[1,192,4096]{2,1,0:T(8,128)(2,1)} copy(bf16[1,192,4096]{2,1,0:T(8,128)(2,1)} %get-tuple-element.4) | data formatting | bytes 3145728
  97.0 0.0 copy-done
  97.0 0.6 copy.15
Async XLA Ops:
  94.3 2.7 %copy-start = (bf16[8,4096]{1,0:T(8,128)(2,1)S(1)}, bf16[8,4096]{1,0:T(8,128)(2,1)}, u32[]{:S(2)}) copy-start(bf16[8,4096]{1,0:T(8,128)(2,1)} %get-tuple-element.5) | copy-start | bytes 196612

commit v4 on v3

--- a/solution.py
+++ b/solution.py
@@ -439,12 +439,12 @@
     next(hids)
     step_n(5)
     next(hids)
-    step_w(0)
-    step_w(1)
     step_n(6)
     step_n(7)
     acc[...] = jnp.zeros_like(acc)
     lax.fori_loop(0, 9, multiply_near, 0, unroll=3)
+    step_w(0)
+    step_w(1)
     step_w(2)
     step_w(3)
     step_w(4)

time: 97.8 us -> 101 us (1.033)
  Pallas kernels: 93.6 us -> 97 us
    pallas_call x1, Pallas kernels: 93.6 us -> 97 us  [local(): pl.pallas_call(kernel, out_shape=(jax.ShapeDtypeStruct((1, ROWS, D), BF),...]
where the time goes in v4:
time: 101 us
  Pallas kernels  97 us (96%)
  local copies, waits for them, and re-layouts  3.37 us (3%)
    pallas_call x1, Pallas kernels, local(): pl.pallas_call(kernel, out_shape=(jax.ShapeDtypeStruct((1, ROWS, D), BF),...  97 us
    unnamed x4, local copies, waits for them, and re-layouts  3.37 us

profile of v4, /device:TPU:1, one launch (start us, length us, event | category | flops | bytes accessed | tf_op | source)
XLA Modules:
  0.0 101.0 jit_solution(4345119029812615697)
XLA Ops:
  0.6 97.0 %shard_map.113 = (bf16[1,192,4096]{2,1,0:T(8,128)(2,1)}, bf16[8,4096]{1,0:T(8,128)(2,1)}) custom-call(s32[32]{0:T(128)} %omap.1, bf16[8,4096]{1,0:T(8,128)(2,1)} %tokens.1, s32[8,8]{1,0:T(8,128)} %ids.1, f32[8,8]{1,0:T(8,128)} %gates.1, f32[1,32,768,128]{3,2,1,0:T(8,128)} %grads.1, f32[32,192,128]{2,1,0:T(8,128)} %master.1, f32[32,192,128]{2,1,0:T(8,128)} %mom1.1, ...), custom_call_target="tpu_custom_call" | custom-call | tf_op jit(solution)/shard_map/pallas_call | solution.py:517
  97.7 0.0 copy-start
  97.7 2.7 %copy.14 = bf16[1,192,4096]{2,1,0:T(8,128)(2,1)} copy(bf16[1,192,4096]{2,1,0:T(8,128)(2,1)} %get-tuple-element.4) | data formatting | bytes 3145728
  100.4 0.0 copy-done
  100.4 0.6 copy.15
Async XLA Ops:
  97.7 2.7 %copy-start = (bf16[8,4096]{1,0:T(8,128)(2,1)S(1)}, bf16[8,4096]{1,0:T(8,128)(2,1)}, u32[]{:S(2)}) copy-start(bf16[8,4096]{1,0:T(8,128)(2,1)} %get-tuple-element.5) | copy-start | bytes 196612
